TPU v7x, 32 devices: a whole 2x2x4 slice. The times are simulated.
32 devices in a mesh: seq: 8 (over z, core), chan: 4 (over y, x).
Axes of the slice: x: 2, y: 2, z: 4, core: 2. Of those that a mesh axis runs over, the one named last changes fastest.
Arguments:
- hyena_in: bfloat16 [2048, 3, 4096], P('seq', None, 'chan'), may hold values from -6 to 6
- prior_kv: bfloat16 [127, 4096], P(None, 'chan'), may hold values from -6 to 6
- filters: float32 [256, 128], P('chan'), may hold values from -0.5 to 0.5
- gain: float32 [4096], replicated, may hold values from 0.5 to 1.5
- w_qkv: bfloat16 [4096, 3, 4096], P('seq', None, 'chan'), may hold values from -0.09375 to 0.09375
- cache_k: bfloat16 [1216, 4096], P('seq', 'chan'), may hold values from -110 to 110
- cache_v: bfloat16 [1216, 4096], P('seq', 'chan'), may hold values from -6 to 6
Outputs:
- attn_out: bfloat16 [2048, 4096], P('seq', 'chan')
All inputs are finite; a program needn't handle non-finite values.
Results may differ from a plain program's by a relative error of at most 0.019.
The roundings to bfloat16 on the way count: a program that leaves them out, or rounds other values in their place, can miss the bound.
Values may be sent and summed in bfloat16 or wider, within the bound.
No kernel may reach another device: no remote copies, remote signals or barrier semaphores. Data moves between devices by JAX's collectives and lax.ppermute only.
A program may use at most 128 MiB of HBM per device.

v0:
```python
import jax
import jax.numpy as jnp
from jax import lax
from jax.sharding import PartitionSpec as P

D = 4096
HEADS = 32


def shifted(value, axis, steps):
    count = lax.axis_size(axis)
    leading, last = (max(0, -steps), min(count, count - steps))
    return lax.ppermute(value, axis, [(source, source + steps) for source in range(leading, last)])


def body(hyena_in, prior_kv, filters, gain, w_qkv, cache_k, cache_v):
    rows_dev = hyena_in.shape[0]
    width = hyena_in.shape[2]
    history = prior_kv.shape[0]
    tap_count = filters.shape[1]
    head_size = D // HEADS
    heads_dev = width // head_size
    cache_rows = cache_k.shape[0]
    stride = cache_rows + rows_dev
    my_index = lax.axis_index("seq")
    stream_q = hyena_in[:, 0].astype(jnp.float32)
    kv_prod = (hyena_in[:, 1].astype(jnp.float32) * hyena_in[:, 2].astype(jnp.float32)).astype(
        jnp.bfloat16
    )
    before = shifted(kv_prod[rows_dev - history :], "seq", 1)
    before = jnp.where(my_index == 0, prior_kv, before)
    extended = jnp.concatenate([before, kv_prod], axis=0).astype(jnp.float32)
    tap_table = jnp.repeat(filters, width // filters.shape[0], axis=0).T

    def add_tap(tap_index, total):
        offset = (tap_count - 1 - tap_index).astype(jnp.int32)
        window = lax.dynamic_slice_in_dim(extended, offset, rows_dev, 0)
        coeff = lax.dynamic_index_in_dim(tap_table, tap_index.astype(jnp.int32), 0, keepdims=True)
        return total + coeff * window

    conv = lax.fori_loop(0, tap_count, add_tap, jnp.zeros((rows_dev, width), jnp.float32))
    hyena_out = (stream_q * conv).astype(jnp.bfloat16)
    whole = lax.all_gather(hyena_out, "chan", axis=1, tiled=True)
    as_float = whole.astype(jnp.float32)
    mean_sq = jnp.mean(as_float * as_float, axis=-1, keepdims=True)
    normed = (as_float * lax.rsqrt(mean_sq + 1e-06) * gain[None, :]).astype(jnp.bfloat16)
    piece = lax.all_gather(w_qkv, "seq", axis=0, tiled=True)
    flat_piece = piece.reshape(piece.shape[0], 3 * width)
    projected = jnp.dot(normed, flat_piece, preferred_element_type=jnp.float32)
    qkv = projected.astype(jnp.bfloat16).reshape(rows_dev, 3, width)
    scale = 1.0 / head_size**0.5
    keys_local = jnp.concatenate([cache_k, qkv[:, 1]], axis=0)
    vals_local = jnp.concatenate([cache_v, qkv[:, 2]], axis=0)
    head_q = qkv[:, 0].reshape(rows_dev, heads_dev, head_size)
    query_pos = my_index * rows_dev + jnp.arange(rows_dev, dtype=jnp.int32)
    run_max = jnp.full((heads_dev, rows_dev), -1e30, jnp.float32)
    key_piece = lax.all_gather(keys_local, "seq", axis=0, tiled=True)
    val_piece = lax.all_gather(vals_local, "seq", axis=0, tiled=True)
    count = key_piece.shape[0]
    row_ids = jnp.arange(count, dtype=jnp.int32)
    source = row_ids // stride
    within = row_ids % stride
    key_pos = jnp.where(within < cache_rows, -1, source * rows_dev + within - cache_rows)
    visible = (key_pos[None, :] <= query_pos[:, None])[None]
    scores = (
        jnp.einsum(
            "qhd,khd->hqk",
            head_q,
            key_piece.reshape(count, heads_dev, head_size),
            preferred_element_type=jnp.float32,
        )
        * scale
    )
    scores = jnp.where(visible, scores, jnp.float32(-1e30))
    new_max = jnp.maximum(run_max, jnp.max(scores, axis=-1))
    weights = jnp.where(visible, jnp.exp(scores - new_max[..., None]), jnp.float32(0.0))
    new_sum = jnp.sum(weights, axis=-1)
    probs = weights.astype(jnp.bfloat16)
    added = jnp.einsum(
        "hqk,khd->hqd",
        probs,
        val_piece.reshape(count, heads_dev, head_size),
        preferred_element_type=jnp.float32,
    )
    result = jnp.transpose(added / new_sum[..., None], (1, 0, 2))
    return result.reshape(rows_dev, width).astype(jnp.bfloat16)


def solution(mesh):
    return jax.shard_map(
        body,
        mesh=mesh,
        in_specs=(
            P("seq", None, "chan"),
            P(None, "chan"),
            P("chan", None),
            P(),
            P("seq", None, "chan"),
            P("seq", "chan"),
            P("seq", "chan"),
        ),
        out_specs=P("seq", "chan"),
        check_vma=False,
    )
```

profile of v0, /device:TPU:0, one launch (start us, length us, event | category | flops | bytes accessed | tf_op | source)
XLA Modules:
  0.0 529.9 jit_solution(969963067514597799)
XLA Ops:
  6.5 1.4 multiply_convert_fusion
  8.0 2.4 collective-permute-start
  10.4 0.8 broadcast_in_dim.41
  11.4 1.4 fusion.38
  12.8 1.0 broadcast_select_fusion
  14.0 71.3 %while.16 = (s32[]{:T(128)}, f32[256,1024]{1,0:T(8,128)S(1)}, f32[128,1024]{1,0:T(8,128)S(1)}, f32[383,1024]{1,0:T(8,128)S(1)}, s32[]{:T(128)}, /*index=5*/s32[]{:T(128)}, s32[]{:T(128)}, s32[]{:T(128)}) while((s32[]{:T(128)}, f32[256,1024]{1,0:T(8,128)S(1)}, f32[128,1024]{1,0:T(8,128)S(1)}, f32[383,1024]{1,0:T(8,128)S(1)}, ...), condition=%wide.region_1.2_spmd.clone, body=%wide.region_0.1_spmd.clone.sunk | while | flops 786439 | bytes 3158165 | solution.py:41
  16.3 0.5 select_add_fusion.2
  16.8 0.5 select_add_fusion.2
  17.4 0.5 select_add_fusion.2
  17.9 0.5 select_add_fusion.2
  21.8 0.5 select_add_fusion.2
  22.4 0.5 select_add_fusion.2
  22.9 0.5 select_add_fusion.2
  26.8 0.5 select_add_fusion.2
  27.4 0.5 select_add_fusion.2
  28.0 0.5 select_add_fusion.2
  28.5 0.5 select_add_fusion.2
  32.4 0.5 select_add_fusion.2
  33.0 0.5 select_add_fusion.2
  33.5 0.5 select_add_fusion.2
  37.4 0.5 select_add_fusion.2
  38.0 0.5 select_add_fusion.2
  38.5 0.5 select_add_fusion.2
  39.1 0.5 select_add_fusion.2
  43.0 0.5 select_add_fusion.2
  43.5 0.5 select_add_fusion.2
  44.1 0.5 select_add_fusion.2
  48.0 0.5 select_add_fusion.2
  48.6 0.5 select_add_fusion.2
  49.1 0.5 select_add_fusion.2
  85.3 2.0 fusion.15
  87.4 4.7 copy.11
  92.1 35.3 %all-gather.5.cloned.1.call-done = bf16[256,4096]{1,0:T(8,128)(2,1)} async-done(((bf16[256,1024]{1,0:T(8,128)(2,1)}), bf16[256,4096]{1,0:T(8,128)(2,1)}) %all-gather.5.cloned.1.call-update) | async-done | bytes 2097168 | tf_op jit(solution)/shard_map/all_gather | solution.py:43
  127.4 2.1 fusion.6
  129.5 219.4 %all-gather.7.cloned.1.call-done = bf16[4096,3,1024]{0,2,1:T(8,128)(2,1)} async-done(((bf16[512,3,1024]{0,2,1:T(8,128)(2,1)}), bf16[4096,3,1024]{0,2,1:T(8,128)(2,1)}) %all-gather.7.cloned.1.call-update) | async-done | bytes 25165840 | tf_op jit(solution)/shard_map/all_gather | solution.py:47
  348.9 12.2 %convolution_convert_fusion = bf16[256,3072]{1,0:T(8,128)(2,1)S(1)} fusion(bf16[4096,3072]{0,1:T(8,128)(2,1)} %bitcast.40, bf16[256,4096]{1,0:T(8,128)(2,1)} %all-gather.5.cloned.1.call-done, f32[4096]{0:T(1024)S(1)} %copy-done.1, f32[256]{0:T(256)S(1)} %add_rsqrt_fusion), kind=kOutput, calls=%fused_computation.14 | convolution fusion | flops 6447431680 | bytes 28853248 | tf_op jit(solution)/shard_map/dot_general | solution.py:49
  361.1 0.7 copy.12
  362.2 1.0 pad_maximum_fusion.1
  363.6 1.9 pad_maximum_fusion
  365.6 1.5 broadcast_compare_fusion
  367.1 62.4 %all-gather.9.cloned.1.call-done = bf16[3264,1024]{1,0:T(8,128)(2,1)} async-done(((bf16[408,1024]{1,0:T(8,128)(2,1)}), bf16[3264,1024]{1,0:T(8,128)(2,1)}) %all-gather.9.cloned.1.call-update) | async-done | bytes 6684688 | tf_op jit(solution)/shard_map/all_gather | solution.py:57
  429.5 9.5 %copy.14 = bf16[3264,1024]{0,1:T(8,128)(2,1)} copy(bf16[3264,1024]{1,0:T(8,128)(2,1)} %all-gather.9.cloned.1.call-done) | data formatting | bytes 13369344 | tf_op jit(solution)/shard_map/all_gather | solution.py:57
  439.0 15.2 %fusion = (f32[8,256]{1,0:T(8,128)S(1)}, f32[8,256,3264]{1,2,0:T(8,128)}) fusion(pred[256,3264]{0,1:T(8,128)(4,1)S(1)} %broadcast_compare_fusion, bf16[256,8,128]{0,2,1:T(8,128)(2,1)S(1)} %bitcast.33, bf16[3264,8,128]{0,2,1:T(8,128)(2,1)} %bitcast.30), kind=kOutput, calls=%fused_computation.4 | convolution fusion | flops 1731328000 | bytes 34791424 | tf_op jit(solution)/shard_map/qhd,khd->hqk/dot_general | solution.py:66
  454.2 12.0 %fusion.1 = f32[8,256]{1,0:T(8,128)S(1)} fusion(f32[8,256,3264]{1,2,0:T(8,128)} %get-tuple-element.147, f32[8,256]{1,0:T(8,128)S(1)} %broadcast_maximum_fusion, pred[256,3264]{0,1:T(8,128)(4,1)S(1)} %broadcast_compare_fusion), kind=kLoop, calls=%fused_computation.5 | loop fusion | flops 33421312 | bytes 27590656 | tf_op jit(solution)/shard_map/reduce_sum | solution.py:77
  466.2 31.5 %all-gather.11.cloned.1.call-done = bf16[3264,1024]{1,0:T(8,128)(2,1)} async-done(((bf16[408,1024]{1,0:T(8,128)(2,1)}), bf16[3264,1024]{1,0:T(8,128)(2,1)}) %all-gather.11.cloned.1.call-update) | async-done | bytes 6684688 | tf_op jit(solution)/shard_map/all_gather | solution.py:58
  497.7 9.4 %copy.18 = bf16[3264,1024]{0,1:T(8,128)(2,1)} copy(bf16[3264,1024]{1,0:T(8,128)(2,1)} %all-gather.11.cloned.1.call-done) | data formatting | bytes 13369344 | tf_op jit(solution)/shard_map/all_gather | solution.py:58
  507.1 15.3 %divide_convert_fusion = bf16[256,8,128]{0,2,1:T(8,128)(2,1)S(1)} fusion(bf16[3264,8,128]{0,2,1:T(8,128)(2,1)} %bitcast.31, f32[8,256,3264]{1,2,0:T(8,128)} %get-tuple-element.147, f32[8,256]{1,0:T(8,128)S(1)} %broadcast_maximum_fusion, pred[256,3264]{0,1:T(8,128)(4,1)S(1)} %broadcast_compare_fusion, f32[256,8]{0,1:T(8,128)S(1)} %bitcast.39), kind=kOutput, calls=%fused_computation.21 | convolution fusion | flops 1745223680 | bytes 34799616 | tf_op jit(solution)/shard_map/hqk,khd->hqd/dot_general | solution.py:79
  522.4 1.0 copy.20
  (256 shorter events, 55.7 us)
Async XLA Ops:
  6.5 120.9 %all-gather.5.cloned.1.call-start = ((), (), s32[]{:S(2)}) async-start(), calls=%async_computation | async-start | bytes 2621440 | tf_op jit(solution)/shard_map/all_gather | solution.py:43
  8.0 4.8 collective-permute-start
  85.3 263.6 %copy-start.1 = (f32[4096]{0:T(1024)S(1)}, f32[4096]{0:T(1024)}, u32[]{:S(2)}) copy-start(f32[4096]{0:T(1024)} %param.12) | copy-start | bytes 49156
  87.3 261.6 %all-gather.7.cloned.1.call-start = ((), (), s32[]{:S(2)}) async-start(), calls=%async_computation.1 | async-start | bytes 28311552 | tf_op jit(solution)/shard_map/all_gather | solution.py:47
  92.1 337.5 %all-gather.9.cloned.1.call-start = ((), (), s32[]{:S(2)}) async-start(), calls=%async_computation.2 | async-start | bytes 7520256 | tf_op jit(solution)/shard_map/all_gather | solution.py:57
  361.1 1.0 copy-start
  363.2 134.5 %all-gather.11.cloned.1.call-start = ((), (), s32[]{:S(2)}) async-start(), calls=%async_computation.3 | async-start | bytes 7520256 | tf_op jit(solution)/shard_map/all_gather | solution.py:58
Sparse Core Ops, SparseCore 0:
  87.4 39.9 all-gather.4
  129.0 219.8 all-gather.6
  363.3 66.1 all-gather.8
  431.0 66.6 all-gather.10
where the time goes:
time: 531 us; the launch traced here: 530 us
  waiting for transfers between devices  349 us (66%)
  other arithmetic  89.5 us (17%)
  matrix products  42.7 us (8%)
  local copies, waits for them, and re-layouts  28.3 us (5%)
  between operations  13.3 us (3%)
    all_gather x1, waiting for transfers between devices, body(): piece = lax.all_gather(w_qkv, 'seq', axis=0, tiled=True)  219 us
    add x128, other arithmetic, add_tap(): return total + coeff * window  65.1 us
    all_gather x1, waiting for transfers between devices, body(): key_piece = lax.all_gather(keys_local, 'seq', axis=0, tiled=True)  62.4 us
    all_gather x1, waiting for transfers between devices, body(): whole = lax.all_gather(hyena_out, 'chan', axis=1, tiled=True)  35.3 us
    all_gather x1, waiting for transfers between devices, body(): val_piece = lax.all_gather(vals_local, 'seq', axis=0, tiled=True)  31.5 us
    dot_general x1, matrix products, body(): jnp.einsum('hqk,khd->hqd', probs, val_piece.reshape(count, heads_dev, hea...  15.3 us
    dot_general x1, matrix products, body(): jnp.einsum('qhd,khd->hqk', head_q, key_piece.reshape(count, heads_dev, he...  15.2 us
    dot_general x1, matrix products, body(): projected = jnp.dot(normed, flat_piece, preferred_element_type=jnp.float32)  12.2 us
  transfers between devices with their start and end apart: 5, of which 4 were waited for; matrix products, arithmetic and copies ran while one was open for 9% of the time, Pallas kernels for 0%

commit v1 on v0

--- a/solution.py
+++ b/solution.py
@@ -1,10 +1,316 @@
+import functools
+
 import jax
 import jax.numpy as jnp
 from jax import lax
+from jax.experimental import pallas as pl
+from jax.experimental.pallas import tpu as pltpu
 from jax.sharding import PartitionSpec as P
 
 D = 4096
 HEADS = 32
+HEAD = D // HEADS
+LANES = 128
+BF16 = jnp.bfloat16
+F32 = jnp.float32
+VMEM_LIMIT = 56 * 1024 * 1024
+
+
+def whole(shape):
+    return pl.BlockSpec(shape, lambda *_: (0,) * len(shape))
+
+
+def conv_kernel(group, hin_ref, halo_ref, taps_ref, out_ref):
+    taps = taps_ref[...]
+    count = taps.shape[0]
+    width = taps.shape[1]
+    kv = (hin_ref[1].astype(F32) * hin_ref[2].astype(F32)).astype(BF16)
+    ext = jnp.concatenate([halo_ref[...], kv], axis=0)
+    rows = kv.shape[0]
+    blocks = rows // width
+    windows = jnp.concatenate(
+        [ext[b * width : (b + 2) * width] for b in range(blocks)], axis=1
+    )
+    high = taps.astype(BF16)
+    low = (taps - high.astype(F32)).astype(BF16)
+    source = lax.broadcasted_iota(jnp.int32, (width, 2 * width), 0)
+    column = lax.broadcasted_iota(jnp.int32, (width, 2 * width), 1)
+    flip = jnp.where(source + column == width, 1.0, 0.0).astype(BF16)
+    total = None
+    for part in (high, low):
+        first = jnp.dot(part, flip, preferred_element_type=F32)
+        toeplitz = jnp.concatenate(
+            [
+                pltpu.roll(
+                    jnp.broadcast_to(first[g : g + 1], (width, 2 * width)),
+                    0,
+                    1,
+                    stride=1,
+                    stride_axis=0,
+                ).astype(BF16)
+                for g in range(count)
+            ],
+            axis=0,
+        )
+        product = jnp.dot(toeplitz, windows, preferred_element_type=F32)
+        total = product if total is None else total + product
+    owner = lax.broadcasted_iota(jnp.int32, (width, blocks * LANES), 1) % LANES // group
+    conv = total[:width]
+    for g in range(1, count):
+        conv = jnp.where(owner == g, total[g * width : (g + 1) * width], conv)
+    query = hin_ref[0].astype(F32)
+    for b in range(blocks):
+        piece = query[b * width : (b + 1) * width] * conv[:, b * LANES : (b + 1) * LANES]
+        out_ref[b * width : (b + 1) * width, :] = piece.astype(BF16)
+
+
+def hyena(hin, halo, filters):
+    _, rows, width = hin.shape
+    taps = filters.shape[1]
+    group = width // filters.shape[0]
+    per_tile = LANES // group
+    return pl.pallas_call(
+        functools.partial(conv_kernel, group),
+        grid=(width // LANES,),
+        in_specs=[
+            pl.BlockSpec((3, rows, LANES), lambda i: (0, 0, i)),
+            pl.BlockSpec((taps, LANES), lambda i: (0, i)),
+            pl.BlockSpec((per_tile, taps), lambda i: (i, 0)),
+        ],
+        out_specs=pl.BlockSpec((rows, LANES), lambda i: (0, i)),
+        out_shape=jax.ShapeDtypeStruct((rows, width), BF16),
+        compiler_params=pltpu.CompilerParams(vmem_limit_bytes=VMEM_LIMIT),
+        name="hyena_filters",
+    )(hin, halo, filters)
+
+
+def norm_kernel(place_ref, own_ref, x_ref, y_ref, d0_ref, d1_ref, gain_ref, out_ref):
+    chan = place_ref[0]
+    half = d0_ref.shape[0]
+    rows = own_ref.shape[0]
+    for part in range(rows // half):
+        band = pl.ds(part * half, half)
+        diag_ref = (d0_ref, d1_ref)[part]
+        parts = [
+            own_ref[band, :].astype(F32),
+            x_ref[band, :].astype(F32),
+            y_ref[band, :].astype(F32),
+            diag_ref[...].astype(F32),
+        ]
+        total = sum(jnp.sum(p * p, axis=-1, keepdims=True) for p in parts)
+        factor = lax.rsqrt(total / D + 1e-6)
+        for m, p in enumerate(parts):
+            where = chan ^ m
+            out_ref[where, band, :] = (p * factor * gain_ref[where]).astype(BF16)
+
+
+def norm(place, own, from_x, from_y, diag0, diag1, gain):
+    rows, width = own.shape
+    half = diag0.shape[0]
+    return pl.pallas_call(
+        norm_kernel,
+        in_specs=[pl.BlockSpec(memory_space=pltpu.SMEM)]
+        + [whole((rows, width))] * 3
+        + [whole((half, width))] * 2
+        + [whole((4, 1, width))],
+        out_specs=whole((4, rows, width)),
+        out_shape=jax.ShapeDtypeStruct((4, rows, width), BF16),
+        compiler_params=pltpu.CompilerParams(vmem_limit_bytes=VMEM_LIMIT),
+        name="norm",
+    )(place, own, from_x, from_y, diag0, diag1, gain)
+
+
+def project_kernel(shift, last, zs, place_ref, *refs):
+    normed, (own_ref, sib_ref), rest = refs[:zs], refs[zs : zs + 2], refs[zs + 2 :]
+    before_ref = rest[0] if len(rest) == 2 else None
+    out_ref = rest[-1]
+    core = place_ref[2]
+    block = lax.rem(place_ref[1] + zs - shift, zs)
+    rows = normed[0].shape[1]
+    depth = normed[0].shape[2] // 2
+    cols = own_ref.shape[1]
+    for j in range(zs):
+        for p in range(3):
+            total = None
+            for k, w_ref in enumerate((own_ref, sib_ref)):
+                at = pl.multiple_of((core ^ k) * depth, depth)
+                left = normed[j][block, :, pl.ds(at, depth)]
+                right = w_ref[p * depth : (p + 1) * depth, :]
+                term = jnp.dot(left, right, preferred_element_type=F32)
+                total = term if total is None else total + term
+            if before_ref is not None:
+                total = total + before_ref[j, :, p * cols : (p + 1) * cols]
+            out_ref[j, :, p * cols : (p + 1) * cols] = total.astype(out_ref.dtype)
+
+
+def project(shift, last, place, normed, own, sib, before):
+    zs = len(normed)
+    rows = normed[0].shape[1]
+    cols = own.shape[1]
+    out = (zs, rows, 3 * cols)
+    args = [place, *normed, own, sib] + ([] if before is None else [before])
+    return pl.pallas_call(
+        functools.partial(project_kernel, shift, last, zs),
+        in_specs=[pl.BlockSpec(memory_space=pltpu.SMEM)] + [whole(a.shape) for a in args[1:]],
+        out_specs=whole(out),
+        out_shape=jax.ShapeDtypeStruct(out, BF16 if last else F32),
+        compiler_params=pltpu.CompilerParams(vmem_limit_bytes=VMEM_LIMIT),
+        name="project",
+    )(*args)
+
+
+NT = (((1,), (1,)), ((), ()))
+
+
+def attend_kernel(place_ref, mine_ref, sib_ref, ck_ref, cv_ref, out_ref):
+    z, core = place_ref[1], place_ref[2]
+    zs, rows, _ = mine_ref.shape
+    cols = ck_ref.shape[1]
+    heads = cols // HEAD
+    factor = 1.4426950408889634 / HEAD**0.5
+    low = -1e30
+    row = lax.broadcasted_iota(jnp.int32, (rows, rows), 0)
+    col = lax.broadcasted_iota(jnp.int32, (rows, rows), 1)
+    causal = col <= row
+    for zq in range(zs):
+        at = [lax.rem(z + zs - b, zs) for b in range(zq + 1)]
+        for h in range(heads):
+            q = mine_ref[at[zq], :, h * HEAD : (h + 1) * HEAD]
+            kcol = slice(cols + h * HEAD, cols + (h + 1) * HEAD)
+            vcol = slice(2 * cols + h * HEAD, 2 * cols + (h + 1) * HEAD)
+            kcol_sib = slice(h * HEAD, (h + 1) * HEAD)
+            vcol_sib = slice(cols + h * HEAD, cols + (h + 1) * HEAD)
+            hcol = slice(h * HEAD, (h + 1) * HEAD)
+            scores = [lax.dot_general(q, ck_ref[:, hcol], NT, preferred_element_type=F32)]
+            values = [lambda: cv_ref[:, hcol]]
+            for b in range(zq + 1):
+                s = lax.dot_general(q, mine_ref[at[b], :, kcol], NT, preferred_element_type=F32)
+                if b == zq:
+                    s = jnp.where(causal, s, low)
+                scores.append(s)
+                values.append(lambda b=b: mine_ref[at[b], :, vcol])
+                s = lax.dot_general(q, sib_ref[at[b], :, kcol_sib], NT, preferred_element_type=F32)
+                if b == zq:
+                    s = jnp.where(core == 1, s, low)
+                scores.append(s)
+                values.append(lambda b=b: sib_ref[at[b], :, vcol_sib])
+            top = functools.reduce(
+                jnp.maximum, [jnp.max(s, axis=-1, keepdims=True) for s in scores]
+            )
+            top = top * factor
+            total, summed = None, None
+            for s, value in zip(scores, values):
+                weights = jnp.exp2(s * factor - top)
+                part = jnp.sum(weights, axis=-1, keepdims=True)
+                added = jnp.dot(weights.astype(BF16), value(), preferred_element_type=F32)
+                total = part if total is None else total + part
+                summed = added if summed is None else summed + added
+            out_ref[zq, :, hcol] = (summed / total).astype(BF16)
+
+
+def attend(place, mine, sib, cache_k, cache_v):
+    zs, rows, _ = mine.shape
+    out = (zs, rows, cache_k.shape[1])
+    args = (mine, sib, cache_k, cache_v)
+    return pl.pallas_call(
+        attend_kernel,
+        in_specs=[pl.BlockSpec(memory_space=pltpu.SMEM)] + [whole(a.shape) for a in args],
+        out_specs=whole(out),
+        out_shape=jax.ShapeDtypeStruct(out, BF16),
+        compiler_params=pltpu.CompilerParams(vmem_limit_bytes=VMEM_LIMIT),
+        name="attend",
+    )(place, *args)
+
+
+def join_kernel(place_ref, *refs):
+    pieces, out_ref = refs[:-1], refs[-1]
+    zs = len(pieces)
+    cols = pieces[0].shape[1]
+    for r, piece in enumerate(pieces):
+        at = lax.rem(place_ref[1] + zs - r, zs) * cols
+        out_ref[:, pl.ds(pl.multiple_of(at, cols), cols)] = piece[...]
+
+
+def join(place, pieces):
+    rows, cols = pieces[0].shape
+    out = (rows, cols * len(pieces))
+    return pl.pallas_call(
+        join_kernel,
+        in_specs=[pl.BlockSpec(memory_space=pltpu.SMEM)] + [whole(p.shape) for p in pieces],
+        out_specs=whole(out),
+        out_shape=jax.ShapeDtypeStruct(out, BF16),
+        name="join",
+    )(place, *pieces)
+
+
+def shift_z(value, steps, zs):
+    pairs = [(2 * a + k, 2 * ((a + steps) % zs) + k) for a in range(zs) for k in range(2)]
+    return lax.ppermute(value, "seq", pairs)
+
+
+def swap_core(value, zs):
+    return lax.ppermute(value, "seq", [(2 * a + k, 2 * a + 1 - k) for a in range(zs) for k in range(2)])
+
+
+def swap_chan(value, bit):
+    return lax.ppermute(value, "chan", [(c, c ^ bit) for c in range(4)])
+
+
+def fast_body(hyena_in, prior_kv, filters, gain, w_qkv, cache_k, cache_v):
+    rows, _, width = hyena_in.shape
+    seqs = lax.axis_size("seq")
+    zs = seqs // 2
+    taps = filters.shape[1]
+    cols = width // zs
+    my_seq = lax.axis_index("seq")
+    z, core = my_seq // 2, my_seq % 2
+    chan = lax.axis_index("chan")
+    place = jnp.stack([chan, z, core]).astype(jnp.int32)
+
+    hin = jnp.transpose(hyena_in, (1, 0, 2))
+    tail = (hin[1, rows - taps :].astype(F32) * hin[2, rows - taps :].astype(F32)).astype(BF16)
+    halo = lax.ppermute(tail, "seq", [(s, s + 1) for s in range(seqs - 1)])
+    halo = jnp.where(my_seq == 0, jnp.pad(prior_kv, ((taps - prior_kv.shape[0], 0), (0, 0))), halo)
+
+    depth = w_qkv.shape[0]
+    w_t = jnp.transpose(w_qkv, (1, 0, 2)).reshape(3 * depth, width)
+    weights, caches = [], []
+    for r in range(zs):
+        at = (z + r) % zs * cols
+        parcel = jnp.concatenate(
+            [lax.dynamic_slice_in_dim(a, at, cols, 1) for a in (w_t, cache_k, cache_v)], axis=0
+        )
+        if r:
+            parcel = shift_z(parcel, r, zs)
+        both = (parcel, swap_core(parcel, zs))
+        weights.append(both)
+        caches += [p[3 * depth :] for p in both]
+    crow = cache_k.shape[0]
+    ck = jnp.concatenate([c[:crow] for c in caches], axis=0)
+    cv = jnp.concatenate([c[crow:] for c in caches], axis=0)
+
+    own = hyena(hin, halo, filters)
+    gain4 = gain.reshape(4, 1, width)
+    normed = []
+    half = rows // 2
+    for j in range(zs):
+        from_x, from_y = swap_chan(own, 1), swap_chan(own, 2)
+        diag0 = swap_chan(from_x[:half], 2)
+        diag1 = swap_chan(from_y[half:], 1)
+        normed.append(norm(place, own, from_x, from_y, diag0, diag1, gain4))
+        if j + 1 < zs:
+            own = shift_z(own, 1, zs)
+
+    total = None
+    for r in range(zs):
+        total = project(r, r == zs - 1, place, normed, *weights[r], total)
+    sib = swap_core(total[:, :, cols:], zs)
+    out = attend(place, total, sib, ck, cv)
+    pieces = []
+    for r in range(zs):
+        piece = lax.dynamic_index_in_dim(out, (z + r) % zs, 0, keepdims=False)
+        pieces.append(shift_z(piece, r, zs) if r else piece)
+    return join(place, pieces)
 
 
 def shifted(value, axis, steps):
@@ -87,8 +393,10 @@
 
 
 def solution(mesh):
+    sizes = mesh.shape
+    paired = sizes["chan"] == 4 and HEADS // sizes["chan"] == sizes["seq"]
     return jax.shard_map(
-        body,
+        fast_body if paired else body,
         mesh=mesh,
         in_specs=(
             P("seq", None, "chan"),

time: 531 us -> 295 us (0.56)
  waiting for transfers between devices: 349 us -> 101 us
  starting transfers between devices: 2.68 us -> 94.7 us
  other arithmetic: 89.5 us -> 2.78 us
  Pallas kernels: 0 us -> 69.2 us
  matrix products: 42.7 us -> 0 us
  between operations: 13.3 us -> 0.43 us
    all_gather x4 -> x0, waiting for transfers between devices: 349 us -> none  [the longest x1 219 us: body(): piece = lax.all_gather(w_qkv, 'seq', axis=0, tiled=True)]
    ppermute x1 -> x31, waiting for transfers between devices: 0.01 us -> 101 us  [the longest x9 59 us: shift_z(): return lax.ppermute(value, 'seq', pairs)]
    ppermute x1 -> x31, starting transfers between devices: 2.37 us -> 94.7 us  [the longest x9 70.2 us: shift_z(): return lax.ppermute(value, 'seq', pairs)]
    pallas_call x0 -> x11, Pallas kernels: none -> 69.2 us  [the longest x4 32.3 us: project(): pl.pallas_call(functools.partial(project_kernel, shift, last, zs), in_spe...]
    add x129 -> x0, other arithmetic: 65.1 us -> none  [the longest x128 65.1 us: add_tap(): return total + coeff * window]
    dot_general x3 -> x0, matrix products: 42.7 us -> none  [the longest x1 15.3 us: body(): jnp.einsum('hqk,khd->hqd', probs, val_piece.reshape(count, heads_dev, hea...]
    all_gather x2 -> x0, local copies, waits for them, and re-layouts: 18.9 us -> none  [the longest x1 9.48 us: body(): key_piece = lax.all_gather(keys_local, 'seq', axis=0, tiled=True)]
    reduce_sum x2 -> x0, other arithmetic: 14.1 us -> none  [the longest x1 12 us: body(): new_sum = jnp.sum(weights, axis=-1)]
  transfers between devices with their start and end apart: 5 -> 31, of which waited for: 4 -> 10; matrix products, arithmetic and copies ran while one was open for 9% -> 7% of each run, Pallas kernels for 0% -> 14%
where the time goes in v1:
time: 295 us; the launch traced here: 294 us
  waiting for transfers between devices  101 us (34%)
  starting transfers between devices  94.7 us (32%)
  Pallas kernels  69.2 us (23%)
  local copies, waits for them, and re-layouts  26.7 us (9%)
    ppermute x9, starting transfers between devices, shift_z(): return lax.ppermute(value, 'seq', pairs)  70.2 us
    ppermute x9, waiting for transfers between devices, shift_z(): return lax.ppermute(value, 'seq', pairs)  59 us
    ppermute x16, waiting for transfers between devices, swap_chan(): return lax.ppermute(value, 'chan', [(c, c ^ bit) for c in range(4)])  41.5 us
    pallas_call x4, Pallas kernels, project(): pl.pallas_call(functools.partial(project_kernel, shift, last, zs), in_spe...  32.3 us
    ppermute x16, starting transfers between devices, swap_chan(): return lax.ppermute(value, 'chan', [(c, c ^ bit) for c in range(4)])  21.3 us
    unnamed x61, local copies, waits for them, and re-layouts  16.3 us
    pallas_call x4, Pallas kernels, norm(): pl.pallas_call(norm_kernel, in_specs=[pl.BlockSpec(memory_space=pltpu.SME...  15.6 us
    pallas_call x1, Pallas kernels, attend(): pl.pallas_call(attend_kernel, in_specs=[pl.BlockSpec(memory_space=pltpu.S...  11.3 us
  transfers between devices with their start and end apart: 31, of which 10 were waited for; matrix products, arithmetic and copies ran while one was open for 7% of the time, Pallas kernels for 14%

profile of v1, /device:TPU:0, one launch (start us, length us, event | category | flops | bytes accessed | tf_op | source)
XLA Modules:
  0.0 294.4 jit_solution(8730397523118601582)
XLA Ops:
  1.1 2.4 collective-permute-start
  3.6 1.9 constant_dynamic-update-slice_fusion
  5.5 2.1 constant_dynamic-slice_fusion.2
  8.4 8.0 %hyena_filters.1.own_ref = bf16[256,1024]{1,0:T(8,128)(2,1)} custom-call(bf16[3,256,1024]{2,1,0:T(8,128)(2,1)} %bitcast.20, bf16[128,1024]{1,0:T(8,128)(2,1)} %pad_select_fusion.halo_ref, f32[64,128]{1,0:T(8,128)} %taps_ref.1), custom_call_target="tpu_custom_call" | custom-call | tf_op jit(solution)/shard_map/hyena_filters/pallas_call | solution.py:72
  16.4 4.2 %collective-permute-start.5 = (bf16[256,1024]{1,0:T(8,128)(2,1)}, bf16[256,1024]{1,0:T(8,128)(2,1)S(1)}, u32[]{:S(2)}, u32[]{:S(2)}) collective-permute-start(bf16[256,1024]{1,0:T(8,128)(2,1)} %hyena_filters.1.own_ref), channel_id=1, source_target_pairs={{0,8},{4,12},{8,16},{12,20},{16,24},{20,28},{24,0},{28,4},{1,9},{5... | collective-permute-start | bytes 1572872 | tf_op jit(solution)/shard_map/ppermute | solution.py:248
  20.7 2.1 collective-permute-start.20
  22.7 1.5 collective-permute-start.2
  25.4 1.5 collective-permute-start.1
  27.0 8.7 %collective-permute-done.5.own_ref = bf16[256,1024]{1,0:T(8,128)(2,1)S(1)} collective-permute-done((bf16[256,1024]{1,0:T(8,128)(2,1)}, bf16[256,1024]{1,0:T(8,128)(2,1)S(1)}, u32[]{:S(2)}, u32[]{:S(2)}) %collective-permute-start.5) | collective-permute-done | bytes 524320 | tf_op jit(solution)/shard_map/ppermute | solution.py:248
  35.7 39.0 %collective-permute-start.24 = (bf16[1840,256]{1,0:T(8,128)(2,1)S(1)}, bf16[1840,256]{1,0:T(8,128)(2,1)}, u32[]{:S(2)}, u32[]{:S(2)}) collective-permute-start(bf16[1840,256]{1,0:T(8,128)(2,1)S(1)} %pad_maximum_fusion.2), channel_id=1, source_target_pairs={{0,8},{4,12},{8,16},{12,20},{16,24},{20,28},{24,0},{28,4},{1,9},{5... | collective-permute-start | bytes 2826248 | tf_op jit(solution)/shard_map/ppermute | solution.py:248
  74.9 2.9 collective-permute-start.10
  77.8 1.5 collective-permute-start.7
  79.3 27.5 %collective-permute-done.10.own_ref = bf16[256,1024]{1,0:T(8,128)(2,1)S(1)} collective-permute-done((bf16[256,1024]{1,0:T(8,128)(2,1)S(1)}, bf16[256,1024]{1,0:T(8,128)(2,1)S(1)}, u32[]{:S(2)}, u32[]{:S(2)}) %collective-permute-start.10) | collective-permute-done | bytes 524320 | tf_op jit(solution)/shard_map/ppermute | solution.py:248
  106.9 19.0 %collective-permute-start.15 = (bf16[256,1024]{1,0:T(8,128)(2,1)S(1)}, bf16[256,1024]{1,0:T(8,128)(2,1)S(1)}, u32[]{:S(2)}, u32[]{:S(2)}) collective-permute-start(bf16[256,1024]{1,0:T(8,128)(2,1)S(1)} %collective-permute-done.10.own_ref), channel_id=1, source_target_pairs={{0,8},{4,12},{8,16},{12,20},{16,24},{20,28},{24,0},{28,4},{1,9},{5... | collective-permute-start | bytes 1572872 | tf_op jit(solution)/shard_map/ppermute | solution.py:248
  125.8 12.3 %collective-permute-done.22.refs_4_ = bf16[1840,256]{1,0:T(8,128)(2,1)S(1)} collective-permute-done((bf16[1840,256]{1,0:T(8,128)(2,1)S(1)}, bf16[1840,256]{1,0:T(8,128)(2,1)S(1)}, u32[]{:S(2)}, u32[]{:S(2)}) %collective-permute-start.22) | collective-permute-done | bytes 942112 | tf_op jit(solution)/shard_map/ppermute | solution.py:248
  140.3 1.5 collective-permute-start.3
  141.9 1.6 collective-permute-start.9
  143.4 15.1 %collective-permute-done.4.d1_ref = bf16[128,1024]{1,0:T(8,128)(2,1)S(1)} collective-permute-done((bf16[128,1024]{1,0:T(8,128)(2,1)S(1)}, bf16[128,1024]{1,0:T(8,128)(2,1)S(1)}, u32[]{:S(2)}, u32[]{:S(2)}) %collective-permute-start.4) | collective-permute-done | bytes 262176 | tf_op jit(solution)/shard_map/ppermute | solution.py:256
  158.5 1.5 collective-permute-start.12
  160.1 1.5 collective-permute-start.11
  162.6 1.5 collective-permute-done.9.d1_ref
  164.2 1.5 collective-permute-start.8
  165.7 21.8 %collective-permute-done.8.d0_ref = bf16[128,1024]{1,0:T(8,128)(2,1)S(1)} collective-permute-done((bf16[128,1024]{1,0:T(8,128)(2,1)S(1)}, bf16[128,1024]{1,0:T(8,128)(2,1)S(1)}, u32[]{:S(2)}, u32[]{:S(2)}) %collective-permute-start.8) | collective-permute-done | bytes 262176 | tf_op jit(solution)/shard_map/ppermute | solution.py:256
  192.7 1.5 collective-permute-start.13
  196.9 2.5 collective-permute-done.14.d1_ref
  201.4 1.5 collective-permute-start.18
  203.0 1.6 slice_dynamic-update-slice_fusion.6
  204.6 1.6 slice_dynamic-update-slice_fusion.5
  206.2 3.9 %norm.4.refs_0_ = bf16[4,256,1024]{2,1,0:T(8,128)(2,1)} custom-call(s32[3]{0:T(128)} %pad_add_fusion.place_ref, bf16[256,1024]{1,0:T(8,128)(2,1)} %hyena_filters.1.own_ref, bf16[256,1024]{1,0:T(8,128)(2,1)} %copy-done.6, bf16[256,1024]{1,0:T(8,128)(2,1)} %copy-done.5, bf16[128,1024]{1,0:T(8,128)(2,1)} %copy-done.18, bf16[128,1024]{1,0:T(8,128)(2,1)} %copy-done.17, ...), custom_call_target="tpu_custom_call" | custom-call | tf_op jit(solution)/shard_map/norm/pallas_call | solution.py:110
  210.1 3.9 %norm.5.refs_1_ = bf16[4,256,1024]{2,1,0:T(8,128)(2,1)} custom-call(s32[3]{0:T(128)} %pad_add_fusion.place_ref, bf16[256,1024]{1,0:T(8,128)(2,1)} %copy-done.14, bf16[256,1024]{1,0:T(8,128)(2,1)} %copy-done.8, bf16[256,1024]{1,0:T(8,128)(2,1)} %copy-done.7, bf16[128,1024]{1,0:T(8,128)(2,1)} %copy-done.20, bf16[128,1024]{1,0:T(8,128)(2,1)} %copy-done.19, ...), custom_call_target="tpu_custom_call" | custom-call | tf_op jit(solution)/shard_map/norm/pallas_call | solution.py:110
  214.0 4.0 %norm.6.refs_2_ = bf16[4,256,1024]{2,1,0:T(8,128)(2,1)} custom-call(s32[3]{0:T(128)} %pad_add_fusion.place_ref, bf16[256,1024]{1,0:T(8,128)(2,1)} %copy-done.15, bf16[256,1024]{1,0:T(8,128)(2,1)} %copy-done.11, bf16[256,1024]{1,0:T(8,128)(2,1)} %copy-done.9, bf16[128,1024]{1,0:T(8,128)(2,1)} %collective-permute-done.13.d0_ref, ...), custom_call_target="tpu_custom_call" | custom-call | tf_op jit(solution)/shard_map/norm/pallas_call | solution.py:110
  219.4 3.9 %norm.7.refs_3_ = bf16[4,256,1024]{2,1,0:T(8,128)(2,1)} custom-call(s32[3]{0:T(128)} %pad_add_fusion.place_ref, bf16[256,1024]{1,0:T(8,128)(2,1)} %copy-done.16, bf16[256,1024]{1,0:T(8,128)(2,1)} %copy-done.12, bf16[256,1024]{1,0:T(8,128)(2,1)} %copy-done.10, bf16[128,1024]{1,0:T(8,128)(2,1)} %copy-done.22, bf16[128,1024]{1,0:T(8,128)(2,1)} %copy-done.21, ...), custom_call_target="tpu_custom_call" | custom-call | tf_op jit(solution)/shard_map/norm/pallas_call | solution.py:110
  223.2 7.4 %project.4.refs_6_ = f32[4,256,768]{2,1,0:T(8,128)} custom-call(s32[3]{0:T(128)} %pad_add_fusion.place_ref, bf16[4,256,1024]{2,1,0:T(8,128)(2,1)} %norm.4.refs_0_, bf16[4,256,1024]{2,1,0:T(8,128)(2,1)} %norm.5.refs_1_, bf16[4,256,1024]{2,1,0:T(8,128)(2,1)} %norm.6.refs_2_, bf16[4,256,1024]{2,1,0:T(8,128)(2,1)} %norm.7.refs_3_, bf16[1840,256]{1,0:T(8,128)(2,1)} %copy-done, ...), custom_call_target="tpu_custom_call" | custom-call | tf_op jit(solution)/shard_map/project/pallas_call | solution.py:152
  230.6 8.5 %project.5.refs_6_ = f32[4,256,768]{2,1,0:T(8,128)} custom-call(s32[3]{0:T(128)} %pad_add_fusion.place_ref, bf16[4,256,1024]{2,1,0:T(8,128)(2,1)} %norm.4.refs_0_, bf16[4,256,1024]{2,1,0:T(8,128)(2,1)} %norm.5.refs_1_, bf16[4,256,1024]{2,1,0:T(8,128)(2,1)} %norm.6.refs_2_, bf16[4,256,1024]{2,1,0:T(8,128)(2,1)} %norm.7.refs_3_, ...), custom_call_target="tpu_custom_call" | custom-call | tf_op jit(solution)/shard_map/project/pallas_call | solution.py:152
  239.1 8.4 %project.6.refs_6_ = f32[4,256,768]{2,1,0:T(8,128)} custom-call(s32[3]{0:T(128)} %pad_add_fusion.place_ref, bf16[4,256,1024]{2,1,0:T(8,128)(2,1)} %norm.4.refs_0_, bf16[4,256,1024]{2,1,0:T(8,128)(2,1)} %norm.5.refs_1_, bf16[4,256,1024]{2,1,0:T(8,128)(2,1)} %norm.6.refs_2_, bf16[4,256,1024]{2,1,0:T(8,128)(2,1)} %norm.7.refs_3_, bf16[1840,256]{1,0:T(8,128)(2,1)} %copy-done.3, ...), custom_call_target="tpu_custom_call" | custom-call | tf_op jit(solution)/shard_map/project/pallas_call | solution.py:152
  247.5 8.0 %project.7.mine_ref = bf16[4,256,768]{2,1,0:T(8,128)(2,1)} custom-call(s32[3]{0:T(128)} %pad_add_fusion.place_ref, bf16[4,256,1024]{2,1,0:T(8,128)(2,1)} %norm.4.refs_0_, bf16[4,256,1024]{2,1,0:T(8,128)(2,1)} %norm.5.refs_1_, bf16[4,256,1024]{2,1,0:T(8,128)(2,1)} %norm.6.refs_2_, bf16[4,256,1024]{2,1,0:T(8,128)(2,1)} %norm.7.refs_3_, ...), custom_call_target="tpu_custom_call" | custom-call | tf_op jit(solution)/shard_map/project/pallas_call | solution.py:152
  255.5 1.5 slice.136
  257.1 1.6 slice_dynamic-update-slice_fusion.4
  258.7 1.6 slice_dynamic-update-slice_fusion.3
  260.4 1.6 slice_dynamic-update-slice_fusion.2
  262.0 1.6 slice_dynamic-update-slice_fusion.1
  263.5 1.6 slice_dynamic-update-slice_fusion
  266.2 11.3 %attend.1 = bf16[4,256,256]{2,1,0:T(8,128)(2,1)} custom-call(s32[3]{0:T(128)} %pad_add_fusion.place_ref, bf16[4,256,768]{2,1,0:T(8,128)(2,1)} %project.7.mine_ref, bf16[4,256,512]{2,1,0:T(8,128)(2,1)} %copy-done.13, bf16[1216,256]{1,0:T(8,128)(2,1)} %get-tuple-element.14.ck_ref, bf16[1216,256]{1,0:T(8,128)(2,1)} %get-tuple-element.13.cv_ref), custom_call_target="tpu_custom_call" | custom-call | tf_op jit(solution)/shard_map/attend/pallas_call | solution.py:215
  277.5 1.8 dynamic-slice_bitcast_fusion
  279.3 2.0 collective-permute-start.28
  281.3 5.1 %collective-permute-done.30.refs_3_ = bf16[256,256]{1,0:T(8,128)(2,1)S(1)} collective-permute-done((bf16[256,256]{1,0:T(8,128)(2,1)S(1)}, bf16[256,256]{1,0:T(8,128)(2,1)S(1)}, u32[]{:S(2)}, u32[]{:S(2)}) %collective-permute-start.30) | collective-permute-done | bytes 131104 | tf_op jit(solution)/shard_map/ppermute | solution.py:248
  286.4 5.3 %collective-permute-done.29.refs_2_ = bf16[256,256]{1,0:T(8,128)(2,1)S(1)} collective-permute-done((bf16[256,256]{1,0:T(8,128)(2,1)S(1)}, bf16[256,256]{1,0:T(8,128)(2,1)S(1)}, u32[]{:S(2)}, u32[]{:S(2)}) %collective-permute-start.29) | collective-permute-done | bytes 131104 | tf_op jit(solution)/shard_map/ppermute | solution.py:248
  292.4 2.0 join.1
  (105 shorter events, 19.6 us)
Async XLA Ops:
  1.1 6.5 %collective-permute-start = (bf16[128,1024]{1,0:T(8,128)(2,1)S(1)}, bf16[128,1024]{1,0:T(8,128)(2,1)S(1)}, u32[]{:S(2)}, u32[]{:S(2)}) collective-permute-start(bf16[128,1024]{1,0:T(8,128)(2,1)S(1)} %fusion), channel_id=1, source_target_pairs={{0,4},{4,8},{8,12},{12,16},{16,20},{20,24},{24,28},{1,5},{5,9},{9,... | collective-permute-start | bytes 786440 | tf_op jit(solution)/shard_map/ppermute | solution.py:272
  16.4 6.3 %copy-start.1 = (bf16[256,1024]{1,0:T(8,128)(2,1)S(1)}, bf16[256,1024]{1,0:T(8,128)(2,1)}, u32[]{:S(2)}) copy-start(bf16[256,1024]{1,0:T(8,128)(2,1)} %hyena_filters.1.own_ref) | copy-start | bytes 1572868
  16.4 19.3 %collective-permute-start.5 = (bf16[256,1024]{1,0:T(8,128)(2,1)}, bf16[256,1024]{1,0:T(8,128)(2,1)S(1)}, u32[]{:S(2)}, u32[]{:S(2)}) collective-permute-start(bf16[256,1024]{1,0:T(8,128)(2,1)} %hyena_filters.1.own_ref), channel_id=1, source_target_pairs={{0,8},{4,12},{8,16},{12,20},{16,24},{20,28},{24,0},{28,4},{1,9},{5... | collective-permute-start | bytes 1572872 | tf_op jit(solution)/shard_map/ppermute | solution.py:248
  20.7 57.1 %collective-permute-start.20 = (bf16[1840,256]{1,0:T(8,128)(2,1)S(1)}, bf16[1840,256]{1,0:T(8,128)(2,1)S(1)}, u32[]{:S(2)}, u32[]{:S(2)}) collective-permute-start(bf16[1840,256]{1,0:T(8,128)(2,1)S(1)} %pad_maximum_fusion), channel_id=1, source_target_pairs={{0,24},{4,28},{8,0},{12,4},{16,8},{20,12},{24,16},{28,20},{1,25},{... | collective-permute-start | bytes 2826248 | tf_op jit(solution)/shard_map/ppermute | solution.py:248
  22.7 52.1 %collective-permute-start.2 = (bf16[256,1024]{1,0:T(8,128)(2,1)S(1)}, bf16[256,1024]{1,0:T(8,128)(2,1)S(1)}, u32[]{:S(2)}, u32[]{:S(2)}) collective-permute-start(bf16[256,1024]{1,0:T(8,128)(2,1)S(1)} %copy-done.1), channel_id=1, source_target_pairs={{0,2},{1,3},{2,0},{3,1},{4,6},{5,7},{6,4},{7,5},{8,10},{9,11},{10,... | collective-permute-start | bytes 1572872 | tf_op jit(solution)/shard_map/ppermute | solution.py:256
  24.3 113.8 %collective-permute-start.22 = (bf16[1840,256]{1,0:T(8,128)(2,1)S(1)}, bf16[1840,256]{1,0:T(8,128)(2,1)S(1)}, u32[]{:S(2)}, u32[]{:S(2)}) collective-permute-start(bf16[1840,256]{1,0:T(8,128)(2,1)S(1)} %pad_maximum_fusion.1), channel_id=1, source_target_pairs={{0,16},{4,20},{8,24},{12,28},{16,0},{20,4},{24,8},{28,12},{1,17},{... | collective-permute-start | bytes 2826248 | tf_op jit(solution)/shard_map/ppermute | solution.py:248
  25.4 49.5 %collective-permute-start.1 = (bf16[256,1024]{1,0:T(8,128)(2,1)S(1)}, bf16[256,1024]{1,0:T(8,128)(2,1)S(1)}, u32[]{:S(2)}, u32[]{:S(2)}) collective-permute-start(bf16[256,1024]{1,0:T(8,128)(2,1)S(1)} %copy-done.1), channel_id=1, source_target_pairs={{0,1},{1,0},{2,3},{3,2},{4,5},{5,4},{6,7},{7,6},{8,9},{9,8},{10,11... | collective-permute-start | bytes 1572872 | tf_op jit(solution)/shard_map/ppermute | solution.py:256
  35.7 126.9 %copy-start.14 = (bf16[256,1024]{1,0:T(8,128)(2,1)}, bf16[256,1024]{1,0:T(8,128)(2,1)S(1)}, u32[]{:S(2)}) copy-start(bf16[256,1024]{1,0:T(8,128)(2,1)S(1)} %collective-permute-done.5.own_ref) | copy-start | bytes 1572868
  35.7 104.0 %collective-permute-start.24 = (bf16[1840,256]{1,0:T(8,128)(2,1)S(1)}, bf16[1840,256]{1,0:T(8,128)(2,1)}, u32[]{:S(2)}, u32[]{:S(2)}) collective-permute-start(bf16[1840,256]{1,0:T(8,128)(2,1)S(1)} %pad_maximum_fusion.2), channel_id=1, source_target_pairs={{0,8},{4,12},{8,16},{12,20},{16,24},{20,28},{24,0},{28,4},{1,9},{5... | collective-permute-start | bytes 2826248 | tf_op jit(solution)/shard_map/ppermute | solution.py:248
  74.8 122.1 %copy-start = (bf16[1840,256]{1,0:T(8,128)(2,1)}, bf16[1840,256]{1,0:T(8,128)(2,1)S(1)}, u32[]{:S(2)}) copy-start(bf16[1840,256]{1,0:T(8,128)(2,1)S(1)} %pad_maximum_fusion.3.refs_4_) | copy-start | bytes 2826244
  74.8 131.4 %copy-start.5 = (bf16[256,1024]{1,0:T(8,128)(2,1)}, bf16[256,1024]{1,0:T(8,128)(2,1)S(1)}, u32[]{:S(2)}) copy-start(bf16[256,1024]{1,0:T(8,128)(2,1)S(1)} %collective-permute-done.2.y_ref) | copy-start | bytes 1572868
  74.8 67.0 %collective-permute-start.26 = (bf16[1840,256]{1,0:T(8,128)(2,1)S(1)}, bf16[1840,256]{1,0:T(8,128)(2,1)S(1)}, u32[]{:S(2)}, u32[]{:S(2)}) collective-permute-start(bf16[1840,256]{1,0:T(8,128)(2,1)S(1)} %pad_maximum_fusion.3.refs_4_), channel_id=1, source_target_pairs={{0,4},{4,0},{8,12},{12,8},{16,20},{20,16},{24,28},{28,24},{1,5},{5... | collective-permute-start | bytes 2826248 | tf_op jit(solution)/shard_map/ppermute | solution.py:252
  74.9 113.1 %copy-start.6 = (bf16[256,1024]{1,0:T(8,128)(2,1)}, bf16[256,1024]{1,0:T(8,128)(2,1)S(1)}, u32[]{:S(2)}) copy-start(bf16[256,1024]{1,0:T(8,128)(2,1)S(1)} %collective-permute-done.1.x_ref) | copy-start | bytes 1572868
  74.9 31.9 %collective-permute-start.10 = (bf16[256,1024]{1,0:T(8,128)(2,1)S(1)}, bf16[256,1024]{1,0:T(8,128)(2,1)S(1)}, u32[]{:S(2)}, u32[]{:S(2)}) collective-permute-start(bf16[256,1024]{1,0:T(8,128)(2,1)S(1)} %collective-permute-done.5.own_ref), channel_id=1, source_target_pairs={{0,8},{4,12},{8,16},{12,20},{16,24},{20,28},{24,0},{28,4},{1,9},{5... | collective-permute-start | bytes 1572872 | tf_op jit(solution)/shard_map/ppermute | solution.py:248
  77.8 119.1 %copy-start.2 = (bf16[1840,256]{1,0:T(8,128)(2,1)}, bf16[1840,256]{1,0:T(8,128)(2,1)S(1)}, u32[]{:S(2)}) copy-start(bf16[1840,256]{1,0:T(8,128)(2,1)S(1)} %collective-permute-done.20.refs_4_) | copy-start | bytes 2826244
  77.8 62.5 %collective-permute-start.7 = (bf16[256,1024]{1,0:T(8,128)(2,1)S(1)}, bf16[256,1024]{1,0:T(8,128)(2,1)S(1)}, u32[]{:S(2)}, u32[]{:S(2)}) collective-permute-start(bf16[256,1024]{1,0:T(8,128)(2,1)S(1)} %collective-permute-done.5.own_ref), channel_id=1, source_target_pairs={{0,2},{1,3},{2,0},{3,1},{4,6},{5,7},{6,4},{7,5},{8,10},{9,11},{10,... | collective-permute-start | bytes 1572872 | tf_op jit(solution)/shard_map/ppermute | solution.py:256
  106.9 85.0 %copy-start.15 = (bf16[256,1024]{1,0:T(8,128)(2,1)}, bf16[256,1024]{1,0:T(8,128)(2,1)S(1)}, u32[]{:S(2)}) copy-start(bf16[256,1024]{1,0:T(8,128)(2,1)S(1)} %collective-permute-done.10.own_ref) | copy-start | bytes 1572868
  106.9 54.7 %collective-permute-start.15 = (bf16[256,1024]{1,0:T(8,128)(2,1)S(1)}, bf16[256,1024]{1,0:T(8,128)(2,1)S(1)}, u32[]{:S(2)}, u32[]{:S(2)}) collective-permute-start(bf16[256,1024]{1,0:T(8,128)(2,1)S(1)} %collective-permute-done.10.own_ref), channel_id=1, source_target_pairs={{0,8},{4,12},{8,16},{12,20},{16,24},{20,28},{24,0},{28,4},{1,9},{5... | collective-permute-start | bytes 1572872 | tf_op jit(solution)/shard_map/ppermute | solution.py:248
  138.1 58.7 %copy-start.3 = (bf16[1840,256]{1,0:T(8,128)(2,1)}, bf16[1840,256]{1,0:T(8,128)(2,1)S(1)}, u32[]{:S(2)}) copy-start(bf16[1840,256]{1,0:T(8,128)(2,1)S(1)} %collective-permute-done.22.refs_4_) | copy-start | bytes 2826244
  138.1 23.9 %collective-permute-start.6 = (bf16[256,1024]{1,0:T(8,128)(2,1)S(1)}, bf16[256,1024]{1,0:T(8,128)(2,1)S(1)}, u32[]{:S(2)}, u32[]{:S(2)}) collective-permute-start(bf16[256,1024]{1,0:T(8,128)(2,1)S(1)} %collective-permute-done.5.own_ref), channel_id=1, source_target_pairs={{0,1},{1,0},{2,3},{3,2},{4,5},{5,4},{6,7},{7,6},{8,9},{9,8},{10,11... | collective-permute-start | bytes 1572872 | tf_op jit(solution)/shard_map/ppermute | solution.py:256
  139.7 18.9 %collective-permute-start.4 = (bf16[128,1024]{1,0:T(8,128)(2,1)S(1)}, bf16[128,1024]{1,0:T(8,128)(2,1)S(1)}, u32[]{:S(2)}, u32[]{:S(2)}) collective-permute-start(bf16[128,1024]{1,0:T(8,128)(2,1)S(1)} %slice.129), channel_id=1, source_target_pairs={{0,1},{1,0},{2,3},{3,2},{4,5},{5,4},{6,7},{7,6},{8,9},{9,8},{10,11... | collective-permute-start | bytes 786440 | tf_op jit(solution)/shard_map/ppermute | solution.py:256
  140.3 47.9 %copy-start.7 = (bf16[256,1024]{1,0:T(8,128)(2,1)}, bf16[256,1024]{1,0:T(8,128)(2,1)S(1)}, u32[]{:S(2)}) copy-start(bf16[256,1024]{1,0:T(8,128)(2,1)S(1)} %collective-permute-done.7.y_ref) | copy-start | bytes 1572868
  140.3 19.8 %collective-permute-start.3 = (bf16[128,1024]{1,0:T(8,128)(2,1)S(1)}, bf16[128,1024]{1,0:T(8,128)(2,1)S(1)}, u32[]{:S(2)}, u32[]{:S(2)}) collective-permute-start(bf16[128,1024]{1,0:T(8,128)(2,1)S(1)} %slice.128), channel_id=1, source_target_pairs={{0,2},{1,3},{2,0},{3,1},{4,6},{5,7},{6,4},{7,5},{8,10},{9,11},{10,... | collective-permute-start | bytes 786440 | tf_op jit(solution)/shard_map/ppermute | solution.py:256
  141.8 46.1 %copy-start.4 = (bf16[1840,256]{1,0:T(8,128)(2,1)}, bf16[1840,256]{1,0:T(8,128)(2,1)S(1)}, u32[]{:S(2)}) copy-start(bf16[1840,256]{1,0:T(8,128)(2,1)S(1)} %collective-permute-done.26.refs_5_) | copy-start | bytes 2826244
  141.9 22.3 %collective-permute-start.9 = (bf16[128,1024]{1,0:T(8,128)(2,1)S(1)}, bf16[128,1024]{1,0:T(8,128)(2,1)S(1)}, u32[]{:S(2)}, u32[]{:S(2)}) collective-permute-start(bf16[128,1024]{1,0:T(8,128)(2,1)S(1)} %slice.131), channel_id=1, source_target_pairs={{0,1},{1,0},{2,3},{3,2},{4,5},{5,4},{6,7},{7,6},{8,9},{9,8},{10,11... | collective-permute-start | bytes 786440 | tf_op jit(solution)/shard_map/ppermute | solution.py:256
  158.5 33.4 %copy-start.17 = (bf16[128,1024]{1,0:T(8,128)(2,1)}, bf16[128,1024]{1,0:T(8,128)(2,1)S(1)}, u32[]{:S(2)}) copy-start(bf16[128,1024]{1,0:T(8,128)(2,1)S(1)} %collective-permute-done.4.d1_ref) | copy-start | bytes 786436
  158.5 28.9 %collective-permute-start.12 = (bf16[256,1024]{1,0:T(8,128)(2,1)S(1)}, bf16[256,1024]{1,0:T(8,128)(2,1)S(1)}, u32[]{:S(2)}, u32[]{:S(2)}) collective-permute-start(bf16[256,1024]{1,0:T(8,128)(2,1)S(1)} %collective-permute-done.10.own_ref), channel_id=1, source_target_pairs={{0,2},{1,3},{2,0},{3,1},{4,6},{5,7},{6,4},{7,5},{8,10},{9,11},{10,... | collective-permute-start | bytes 1572872 | tf_op jit(solution)/shard_map/ppermute | solution.py:256
  160.1 31.9 %copy-start.18 = (bf16[128,1024]{1,0:T(8,128)(2,1)}, bf16[128,1024]{1,0:T(8,128)(2,1)S(1)}, u32[]{:S(2)}) copy-start(bf16[128,1024]{1,0:T(8,128)(2,1)S(1)} %collective-permute-done.3.d0_ref) | copy-start | bytes 786436
  160.1 27.9 %collective-permute-start.11 = (bf16[256,1024]{1,0:T(8,128)(2,1)S(1)}, bf16[256,1024]{1,0:T(8,128)(2,1)S(1)}, u32[]{:S(2)}, u32[]{:S(2)}) collective-permute-start(bf16[256,1024]{1,0:T(8,128)(2,1)S(1)} %collective-permute-done.10.own_ref), channel_id=1, source_target_pairs={{0,1},{1,0},{2,3},{3,2},{4,5},{5,4},{6,7},{7,6},{8,9},{9,8},{10,11... | collective-permute-start | bytes 1572872 | tf_op jit(solution)/shard_map/ppermute | solution.py:256
  161.6 30.4 %copy-start.16 = (bf16[256,1024]{1,0:T(8,128)(2,1)}, bf16[256,1024]{1,0:T(8,128)(2,1)S(1)}, u32[]{:S(2)}) copy-start(bf16[256,1024]{1,0:T(8,128)(2,1)S(1)} %collective-permute-done.15.own_ref) | copy-start | bytes 1572868
  161.6 28.0 %collective-permute-start.17 = (bf16[256,1024]{1,0:T(8,128)(2,1)S(1)}, bf16[256,1024]{1,0:T(8,128)(2,1)S(1)}, u32[]{:S(2)}, u32[]{:S(2)}) collective-permute-start(bf16[256,1024]{1,0:T(8,128)(2,1)S(1)} %collective-permute-done.15.own_ref), channel_id=1, source_target_pairs={{0,2},{1,3},{2,0},{3,1},{4,6},{5,7},{6,4},{7,5},{8,10},{9,11},{10,... | collective-permute-start | bytes 1572872 | tf_op jit(solution)/shard_map/ppermute | solution.py:256
  162.1 26.8 %copy-start.8 = (bf16[256,1024]{1,0:T(8,128)(2,1)}, bf16[256,1024]{1,0:T(8,128)(2,1)S(1)}, u32[]{:S(2)}) copy-start(bf16[256,1024]{1,0:T(8,128)(2,1)S(1)} %collective-permute-done.6.x_ref) | copy-start | bytes 1572868
  162.1 29.8 %collective-permute-start.16 = (bf16[256,1024]{1,0:T(8,128)(2,1)S(1)}, bf16[256,1024]{1,0:T(8,128)(2,1)S(1)}, u32[]{:S(2)}, u32[]{:S(2)}) collective-permute-start(bf16[256,1024]{1,0:T(8,128)(2,1)S(1)} %collective-permute-done.15.own_ref), channel_id=1, source_target_pairs={{0,1},{1,0},{2,3},{3,2},{4,5},{5,4},{6,7},{7,6},{8,9},{9,8},{10,11... | collective-permute-start | bytes 1572872 | tf_op jit(solution)/shard_map/ppermute | solution.py:256
  164.2 27.8 %copy-start.19 = (bf16[128,1024]{1,0:T(8,128)(2,1)}, bf16[128,1024]{1,0:T(8,128)(2,1)S(1)}, u32[]{:S(2)}) copy-start(bf16[128,1024]{1,0:T(8,128)(2,1)S(1)} %collective-permute-done.9.d1_ref) | copy-start | bytes 786436
  164.2 23.3 %collective-permute-start.8 = (bf16[128,1024]{1,0:T(8,128)(2,1)S(1)}, bf16[128,1024]{1,0:T(8,128)(2,1)S(1)}, u32[]{:S(2)}, u32[]{:S(2)}) collective-permute-start(bf16[128,1024]{1,0:T(8,128)(2,1)S(1)} %slice.130), channel_id=1, source_target_pairs={{0,2},{1,3},{2,0},{3,1},{4,6},{5,7},{6,4},{7,5},{8,10},{9,11},{10,... | collective-permute-start | bytes 786440 | tf_op jit(solution)/shard_map/ppermute | solution.py:256
  187.5 4.5 %copy-start.20 = (bf16[128,1024]{1,0:T(8,128)(2,1)}, bf16[128,1024]{1,0:T(8,128)(2,1)S(1)}, u32[]{:S(2)}) copy-start(bf16[128,1024]{1,0:T(8,128)(2,1)S(1)} %collective-permute-done.8.d0_ref) | copy-start | bytes 786436
  187.5 43.2 %collective-permute-start.25 = (bf16[1840,256]{1,0:T(8,128)(2,1)}, bf16[1840,256]{1,0:T(8,128)(2,1)}, u32[]{:S(2)}, u32[]{:S(2)}) collective-permute-start(bf16[1840,256]{1,0:T(8,128)(2,1)} %collective-permute-done.24.refs_4_), channel_id=1, source_target_pairs={{0,4},{4,0},{8,12},{12,8},{16,20},{20,16},{24,28},{28,24},{1,5},{5... | collective-permute-start | bytes 2826248 | tf_op jit(solution)/shard_map/ppermute | solution.py:252
  187.5 51.6 %collective-permute-start.23 = (bf16[1840,256]{1,0:T(8,128)(2,1)S(1)}, bf16[1840,256]{1,0:T(8,128)(2,1)}, u32[]{:S(2)}, u32[]{:S(2)}) collective-permute-start(bf16[1840,256]{1,0:T(8,128)(2,1)S(1)} %collective-permute-done.22.refs_4_), channel_id=1, source_target_pairs={{0,4},{4,0},{8,12},{12,8},{16,20},{20,16},{24,28},{28,24},{1,5},{5... | collective-permute-start | bytes 2826248 | tf_op jit(solution)/shard_map/ppermute | solution.py:252
  188.0 59.5 %collective-permute-start.21 = (bf16[1840,256]{1,0:T(8,128)(2,1)S(1)}, bf16[1840,256]{1,0:T(8,128)(2,1)}, u32[]{:S(2)}, u32[]{:S(2)}) collective-permute-start(bf16[1840,256]{1,0:T(8,128)(2,1)S(1)} %collective-permute-done.20.refs_4_), channel_id=1, source_target_pairs={{0,4},{4,0},{8,12},{12,8},{16,20},{20,16},{24,28},{28,24},{1,5},{5... | collective-permute-start | bytes 2826248 | tf_op jit(solution)/shard_map/ppermute | solution.py:252
  190.4 9.0 %collective-permute-start.14 = (bf16[128,1024]{1,0:T(8,128)(2,1)}, bf16[128,1024]{1,0:T(8,128)(2,1)}, u32[]{:S(2)}, u32[]{:S(2)}) collective-permute-start(bf16[128,1024]{1,0:T(8,128)(2,1)} %slice.133), channel_id=1, source_target_pairs={{0,1},{1,0},{2,3},{3,2},{4,5},{5,4},{6,7},{7,6},{8,9},{9,8},{10,11... | collective-permute-start | bytes 786440 | tf_op jit(solution)/shard_map/ppermute | solution.py:256
  192.7 8.7 %collective-permute-start.13 = (bf16[128,1024]{1,0:T(8,128)(2,1)}, bf16[128,1024]{1,0:T(8,128)(2,1)}, u32[]{:S(2)}, u32[]{:S(2)}) collective-permute-start(bf16[128,1024]{1,0:T(8,128)(2,1)} %slice.132), channel_id=1, source_target_pairs={{0,2},{1,3},{2,0},{3,1},{4,6},{5,7},{6,4},{7,5},{8,10},{9,11},{10,... | collective-permute-start | bytes 786440 | tf_op jit(solution)/shard_map/ppermute | solution.py:256
  199.4 18.6 %collective-permute-start.19 = (bf16[128,1024]{1,0:T(8,128)(2,1)S(1)}, bf16[128,1024]{1,0:T(8,128)(2,1)S(1)}, u32[]{:S(2)}, u32[]{:S(2)}) collective-permute-start(bf16[128,1024]{1,0:T(8,128)(2,1)S(1)} %slice.135), channel_id=1, source_target_pairs={{0,1},{1,0},{2,3},{3,2},{4,5},{5,4},{6,7},{7,6},{8,9},{9,8},{10,11... | collective-permute-start | bytes 786440 | tf_op jit(solution)/shard_map/ppermute | solution.py:256
  201.4 16.5 %collective-permute-start.18 = (bf16[128,1024]{1,0:T(8,128)(2,1)S(1)}, bf16[128,1024]{1,0:T(8,128)(2,1)S(1)}, u32[]{:S(2)}, u32[]{:S(2)}) collective-permute-start(bf16[128,1024]{1,0:T(8,128)(2,1)S(1)} %slice.134), channel_id=1, source_target_pairs={{0,2},{1,3},{2,0},{3,1},{4,6},{5,7},{6,4},{7,5},{8,10},{9,11},{10,... | collective-permute-start | bytes 786440 | tf_op jit(solution)/shard_map/ppermute | solution.py:256
  257.0 8.1 %collective-permute-start.27 = (bf16[4,256,512]{2,1,0:T(8,128)(2,1)S(1)}, bf16[4,256,512]{2,1,0:T(8,128)(2,1)S(1)}, u32[]{:S(2)}, u32[]{:S(2)}) collective-permute-start(bf16[4,256,512]{2,1,0:T(8,128)(2,1)S(1)} %slice.136), channel_id=1, source_target_pairs={{0,4},{4,0},{8,12},{12,8},{16,20},{20,16},{24,28},{28,24},{1,5},{5... | collective-permute-start | bytes 3145736 | tf_op jit(solution)/shard_map/ppermute | solution.py:252
  279.3 7.1 %collective-permute-start.30 = (bf16[256,256]{1,0:T(8,128)(2,1)S(1)}, bf16[256,256]{1,0:T(8,128)(2,1)S(1)}, u32[]{:S(2)}, u32[]{:S(2)}) collective-permute-start(bf16[256,256]{1,0:T(8,128)(2,1)S(1)} %get-tuple-element.27), channel_id=1, source_target_pairs={{0,24},{4,28},{8,0},{12,4},{16,8},{20,12},{24,16},{28,20},{1,25},{... | collective-permute-start | bytes 393224 | tf_op jit(solution)/shard_map/ppermute | solution.py:248
  279.3 12.5 %collective-permute-start.29 = (bf16[256,256]{1,0:T(8,128)(2,1)S(1)}, bf16[256,256]{1,0:T(8,128)(2,1)S(1)}, u32[]{:S(2)}, u32[]{:S(2)}) collective-permute-start(bf16[256,256]{1,0:T(8,128)(2,1)S(1)} %get-tuple-element.28), channel_id=1, source_target_pairs={{0,16},{4,20},{8,24},{12,28},{16,0},{20,4},{24,8},{28,12},{1,17},{... | collective-permute-start | bytes 393224 | tf_op jit(solution)/shard_map/ppermute | solution.py:248
  279.3 12.5 %collective-permute-start.28 = (bf16[256,256]{1,0:T(8,128)(2,1)S(1)}, bf16[256,256]{1,0:T(8,128)(2,1)S(1)}, u32[]{:S(2)}, u32[]{:S(2)}) collective-permute-start(bf16[256,256]{1,0:T(8,128)(2,1)S(1)} %get-tuple-element.29), channel_id=1, source_target_pairs={{0,8},{4,12},{8,16},{12,20},{16,24},{20,28},{24,0},{28,4},{1,9},{5... | collective-permute-start | bytes 393224 | tf_op jit(solution)/shard_map/ppermute | solution.py:248
  286.4 5.3 %copy-start.24 = (bf16[256,256]{1,0:T(8,128)(2,1)}, bf16[256,256]{1,0:T(8,128)(2,1)S(1)}, u32[]{:S(2)}) copy-start(bf16[256,256]{1,0:T(8,128)(2,1)S(1)} %collective-permute-done.30.refs_3_) | copy-start | bytes 393220
  (10 other events, 13.5 us)
